TPU v7x, 32 devices: a whole 2x2x4 slice. The times are simulated.
32 devices in a mesh: dp: 4 (over y, core), cent: 8 (over z, x).
Axes of the slice: x: 2, y: 2, z: 4, core: 2. Of those that a mesh axis runs over, the one named last changes fastest.
Arguments:
- fragments: bfloat16 [8192, 1024], P(('dp', 'cent')), may hold values from -1500 to 1500
- order: int32 [32, 256], P(('dp', 'cent')), may hold values from 0 to 255, each once within a row
- group_ids: int32 [8192, 1], P(('dp', 'cent')), may hold values from 0 to 7; in each aligned block of 256 rows (0 to 255, 256 to 511, ...) at most 64 rows name the same one
- w_first: bfloat16 [1024, 1024], replicated, may hold values from -0.1875 to 0.1875
- w_second: bfloat16 [1024, 256], replicated, may hold values from -0.1875 to 0.1875
- centroids: float32 [8192, 256], P('cent'), may hold values from -24 to 24
Outputs:
- centroids_out: float32 [8192, 256], P('cent')
Inputs may be any that keep to these rules, and one draw needn't show every extreme that they name: `order`: each row is a permutation of 0 to 255. `group_ids`: among the rows of one device (aligned blocks of 256 rows) no group is named by more than 64 rows, a bound that some block reaches.
All inputs are finite; a program needn't handle non-finite values.
Results may differ from a plain program's by a relative error of at most 0.0075.
Values may be sent and summed in bfloat16 or wider, within the bound.
A program may use at most 64 MiB of HBM per device.

v0:
```python
import jax
import jax.numpy as jnp
from jax import lax
from jax.sharding import PartitionSpec as P

STEPS = 2


beta_scale = 0.0625
prior_weight = 1.0
eps_value = 1e-05


def per_device(fragments, order, group_ids, w_first, w_second, centroids):
    rows_here = fragments.shape[0]
    picked = jnp.take(fragments, order[0], axis=0)
    hidden = jax.nn.gelu(
        jnp.dot(picked, w_first, preferred_element_type=jnp.float32), approximate=True
    ).astype(jnp.bfloat16)
    proj = jnp.dot(hidden, w_second, preferred_element_type=jnp.float32)
    total_rows = float(rows_here * lax.axis_size("dp") * lax.axis_size("cent"))
    mean = lax.psum(jnp.sum(proj, axis=0), ("dp", "cent")) / total_rows
    var = lax.psum(jnp.sum((proj - mean) ** 2, axis=0), ("dp", "cent")) / total_rows
    zrows = ((proj - mean) * lax.rsqrt(var + eps_value)).astype(jnp.bfloat16)
    width = zrows.shape[1]
    groups = group_ids[:, 0]
    group_count = lax.axis_size("cent")
    capacity = 2 * rows_here // group_count
    member = (groups[:, None] == jnp.arange(group_count, dtype=jnp.int32)[None, :]).astype(
        jnp.float32
    )
    index = jnp.arange(rows_here, dtype=jnp.int32)
    before = (index[:, None] > index[None, :]).astype(jnp.float32)
    rank = jnp.sum(jnp.dot(before, member) * member, axis=1).astype(jnp.int32)
    slot = groups * capacity + rank
    place = (slot[:, None] == jnp.arange(group_count * capacity, dtype=jnp.int32)[None, :]).astype(
        jnp.bfloat16
    )
    packed = lax.dot_general(
        place, zrows, (((0,), (0,)), ((), ())), preferred_element_type=jnp.float32
    ).astype(jnp.bfloat16)
    filled = jnp.sum(place.astype(jnp.float32), axis=0).astype(jnp.bfloat16)
    received, live = (
        lax.all_to_all(
            packed.reshape(group_count, capacity, width),
            "cent",
            split_axis=0,
            concat_axis=0,
            tiled=True,
        ),
        lax.all_to_all(
            filled.reshape(group_count, capacity), "cent", split_axis=0, concat_axis=0, tiled=True
        ),
    )
    received = received.reshape(group_count * capacity, width)
    live_rows = live.reshape(group_count * capacity).astype(jnp.float32)
    current = centroids
    parts_dp = lax.axis_size("dp")
    where_dp = lax.axis_index("dp")
    for step in range(STEPS):
        rounded = current.astype(jnp.bfloat16)
        cnorm = jnp.sum(current * current, axis=1)
        cross = lax.dot_general(
            received, rounded, (((1,), (1,)), ((), ())), preferred_element_type=jnp.float32
        )
        scores = beta_scale * (2.0 * cross - cnorm[None, :])
        top = jnp.max(scores, axis=1, keepdims=True)
        expo = jnp.exp(scores - top)
        resp = (expo / jnp.sum(expo, axis=1, keepdims=True) * live_rows[:, None]).astype(
            jnp.bfloat16
        )
        num = lax.dot_general(
            resp, received, (((0,), (0,)), ((), ())), preferred_element_type=jnp.float32
        )
        den = jnp.sum(resp.astype(jnp.float32), axis=0)
        share = current.shape[0] // parts_dp
        num_part, den_part = (
            lax.psum_scatter(num, "dp", scatter_dimension=0, tiled=True),
            lax.psum_scatter(den, "dp", scatter_dimension=0, tiled=True),
        )
        old = lax.dynamic_slice_in_dim(current, where_dp * share, share, 0)
        fresh = (num_part + prior_weight * old) / (den_part + prior_weight)[:, None]
        current = lax.all_gather(fresh, "dp", axis=0, tiled=True)
    return current


def solution(mesh):
    return jax.shard_map(
        per_device,
        mesh=mesh,
        in_specs=(
            P(("dp", "cent"), None),
            P(("dp", "cent"), None),
            P(("dp", "cent"), None),
            P(),
            P(),
            P("cent", None),
        ),
        out_specs=P("cent", None),
        check_vma=False,
    )
```

profile of v0, /device:TPU:0, one launch (start us, length us, event | category | flops | bytes accessed | tf_op | source)
XLA Modules:
  0.0 222.9 jit_solution(5794457838258072373)
XLA Ops:
  6.5 0.0 copy-start
  6.5 1.0 fusion.2
  7.6 0.7 multiply_add_fusion
  8.3 0.1 fusion.23
  8.4 0.7 all_to_all.12
  9.1 7.3 %all-to-all-start.1 = ((bf16[8,1,64]{2,1,0:T(2,128)(2,1)}), bf16[8,1,64]{2,1,0:T(2,128)(2,1)S(1)}, u32[]{:S(2)}, u32[]{:S(2)}) async-start(bf16[8,1,64]{2,1,0:T(2,128)(2,1)} %all_to_all.12), calls=%async_computation.1 | async-start | bytes 8192 | tf_op jit(solution)/shard_map/all_to_all | solution.py:51
  16.3 0.7 compare_select_fusion
  17.0 0.7 compare_and_fusion
  17.7 3.5 %gather_fusion = bf16[256,1024]{1,0:T(8,128)(2,1)} fusion(bf16[256,1024]{1,0:T(8,128)(2,1)} %param.6, s32[1024]{0:T(1024)S(1)} %pad_clamp_fusion), kind=kCustom, calls=%fused_computation | custom fusion | bytes 1049600 | tf_op jit(solution)/shard_map/jit(_take)/gather | solution.py:16
  21.2 0.0 copy-done
  21.2 0.0 copy-start.1
  21.2 2.4 %fusion.36 = (f32[256]{0:T(256)S(1)}, f32[256,256]{1,0:T(8,128)S(1)}) fusion(bf16[1024,256]{1,0:T(8,128)(2,1)} %param.10, bf16[1024,1024]{1,0:T(8,128)(2,1)S(1)} %copy-done, bf16[256,1024]{1,0:T(8,128)(2,1)} %gather_fusion, pred[256]{0:T(512)(128)(4,1)S(1)} %compare_and_fusion), kind=kOutput, calls=%fused_computation.60 | convolution fusion | flops 673775360 | bytes 3409152 | tf_op jit(solution)/shard_map/dot_general | solution.py:20
  23.6 40.8 %psum.14 = f32[256]{0:T(256)S(1)} all-reduce(f32[256]{0:T(256)S(1)} %get-tuple-element.9), channel_id=1, replica_groups=mesh['dp'=4,'cent'=8] {'dp','cent'}, use_global_device_ids=true, to_apply=%region_2.3 | all-reduce | flops 256 | bytes 2048 | tf_op jit(solution)/shard_map/psum | solution.py:22
  64.5 0.1 multiply_reduce_fusion.2
  64.5 40.0 %psum.15 = f32[256]{0:T(256)S(1)} all-reduce(f32[256]{0:T(256)S(1)} %multiply_reduce_fusion.2), channel_id=1, replica_groups=mesh['dp'=4,'cent'=8] {'dp','cent'}, use_global_device_ids=true, to_apply=%region_4.5 | all-reduce | flops 256 | bytes 2048 | tf_op jit(solution)/shard_map/psum | solution.py:23
  104.6 1.1 convolution_convert_fusion
  105.7 0.0 all-to-all-done.1
  105.7 5.3 %all-to-all-start = ((bf16[8,64,256]{2,1,0:T(8,128)(2,1)}), bf16[8,64,256]{2,1,0:T(8,128)(2,1)S(1)}, u32[]{:S(2)}, u32[]{:S(2)}) async-start(bf16[8,64,256]{2,1,0:T(8,128)(2,1)} %bitcast.22), calls=%async_computation | async-start | bytes 524288 | tf_op jit(solution)/shard_map/all_to_all | solution.py:44
  111.0 0.0 reduce-scatter.3.cloned.1.call-start
  111.0 0.0 copy-done.1
  111.1 0.2 multiply_reduce_fusion.1
  111.3 0.1 reshape.73
  111.4 7.9 %all-to-all-done = bf16[8,64,256]{2,1,0:T(8,128)(2,1)S(1)} async-done(((bf16[8,64,256]{2,1,0:T(8,128)(2,1)}), bf16[8,64,256]{2,1,0:T(8,128)(2,1)S(1)}, u32[]{:S(2)}, u32[]{:S(2)}) %all-to-all-start) | async-done | bytes 262176 | tf_op jit(solution)/shard_map/all_to_all | solution.py:44
  119.3 0.6 fusion.39
  119.9 0.5 fusion
  120.4 0.6 convert_reduce_fusion.1
  121.0 0.0 copy-start.2
  121.0 1.5 fusion.41
  122.5 0.0 reduce-scatter.3.cloned.1.call-update
  122.5 0.0 all-gather.3.cloned.1.call-start
  122.6 0.0 copy-done.2
  122.6 0.6 dynamic-slice
  123.8 5.7 %all-reduce = f32[1024]{0:T(1024)S(1)} all-reduce(f32[1024]{0:T(1024)S(1)} %get-tuple-element.7), channel_id=3, replica_groups=mesh['dp'=4,'cent'=8] {'dp'}, use_global_device_ids=true, to_apply=%region_11.12.clone | all-reduce | flops 1024 | bytes 8192
  129.5 0.1 dynamic-slice_add_fusion.1
  129.6 16.2 %reduce-scatter.3.cloned.1.call-done = f32[256,256]{1,0:T(8,128)} async-done(((f32[1024,256]{1,0:T(8,128)}), f32[256,256]{1,0:T(8,128)}) %reduce-scatter.3.cloned.1.call-update) | async-done | bytes 262160 | tf_op jit(solution)/shard_map/reduce_scatter | solution.py:78
  145.8 1.8 add_divide_fusion.1
  147.6 0.0 all-gather.3.cloned.1.call-update
  147.6 0.0 reduce-scatter.5.cloned.1.call-start
  147.6 16.8 %all-gather.3.cloned.1.call-done = f32[1024,256]{1,0:T(8,128)} async-done(((f32[256,256]{1,0:T(8,128)}), f32[1024,256]{1,0:T(8,128)}) %all-gather.3.cloned.1.call-update) | async-done | bytes 1048592 | tf_op jit(solution)/shard_map/all_gather | solution.py:83
  164.5 1.4 multiply_reduce_fusion
  165.9 1.8 fusion.40
  167.7 0.5 fusion.1
  168.2 0.6 convert_reduce_fusion
  168.9 1.5 fusion.42
  170.3 0.0 reduce-scatter.5.cloned.1.call-update
  170.3 0.0 all-gather.5.cloned.1.call-start
  170.4 5.9 %all-reduce.1 = f32[1024]{0:T(1024)S(1)} all-reduce(f32[1024]{0:T(1024)S(1)} %get-tuple-element.5), channel_id=5, replica_groups=mesh['dp'=4,'cent'=8] {'dp'}, use_global_device_ids=true, to_apply=%region_17.18.clone | all-reduce | flops 1024 | bytes 8192
  176.3 0.1 dynamic-slice_add_fusion
  176.4 19.0 %reduce-scatter.5.cloned.1.call-done = f32[256,256]{1,0:T(8,128)} async-done(((f32[1024,256]{1,0:T(8,128)}), f32[256,256]{1,0:T(8,128)}) %reduce-scatter.5.cloned.1.call-update) | async-done | bytes 262160 | tf_op jit(solution)/shard_map/reduce_scatter | solution.py:78
  195.4 1.8 add_divide_fusion
  197.2 0.0 all-gather.5.cloned.1.call-update
  197.3 16.9 %all-gather.5.cloned.1.call-done = f32[1024,256]{1,0:T(8,128)} async-done(((f32[256,256]{1,0:T(8,128)}), f32[1024,256]{1,0:T(8,128)}) %all-gather.5.cloned.1.call-update) | async-done | bytes 1048592 | tf_op jit(solution)/shard_map/all_gather | solution.py:83
  214.1 2.3 %copy.10 = f32[1024,256]{1,0:T(8,128)} copy(f32[1024,256]{1,0:T(8,128)} %all-gather.5.cloned.1.call-done) | data formatting | bytes 2097152
  (5 shorter events, 0.0 us)
Async XLA Ops:
  6.5 14.7 %copy-start = (bf16[1024,1024]{1,0:T(8,128)(2,1)S(1)}, bf16[1024,1024]{1,0:T(8,128)(2,1)}, u32[]{:S(2)}) copy-start(bf16[1024,1024]{1,0:T(8,128)(2,1)} %param.9) | copy-start | bytes 6291460
  9.1 96.6 %all-to-all-start.1 = ((bf16[8,1,64]{2,1,0:T(2,128)(2,1)}), bf16[8,1,64]{2,1,0:T(2,128)(2,1)S(1)}, u32[]{:S(2)}, u32[]{:S(2)}) async-start(bf16[8,1,64]{2,1,0:T(2,128)(2,1)} %all_to_all.12), calls=%async_computation.1 | async-start | bytes 8192 | tf_op jit(solution)/shard_map/all_to_all | solution.py:51
  21.2 89.9 %copy-start.1 = (f32[1024,256]{1,0:T(8,128)S(1)}, f32[1024,256]{1,0:T(8,128)}, u32[]{:S(2)}) copy-start(f32[1024,256]{1,0:T(8,128)} %param.11) | copy-start | bytes 3145732
  105.7 13.6 %all-to-all-start = ((bf16[8,64,256]{2,1,0:T(8,128)(2,1)}), bf16[8,64,256]{2,1,0:T(8,128)(2,1)S(1)}, u32[]{:S(2)}, u32[]{:S(2)}) async-start(bf16[8,64,256]{2,1,0:T(8,128)(2,1)} %bitcast.22), calls=%async_computation | async-start | bytes 524288 | tf_op jit(solution)/shard_map/all_to_all | solution.py:44
  111.0 34.8 %reduce-scatter.3.cloned.1.call-start = ((), (), s32[]{:S(2)}) async-start(), calls=%async_computation.4 | async-start | bytes 1310720 | tf_op jit(solution)/shard_map/reduce_scatter | solution.py:78
  121.0 1.5 copy-start.2
  122.5 42.0 %all-gather.3.cloned.1.call-start = ((), (), s32[]{:S(2)}) async-start(), calls=%async_computation.5 | async-start | bytes 1310720 | tf_op jit(solution)/shard_map/all_gather | solution.py:83
  147.6 47.8 %reduce-scatter.5.cloned.1.call-start = ((), (), s32[]{:S(2)}) async-start(), calls=%async_computation.6 | async-start | bytes 1310720 | tf_op jit(solution)/shard_map/reduce_scatter | solution.py:78
  170.3 43.8 %all-gather.5.cloned.1.call-start = ((), (), s32[]{:S(2)}) async-start(), calls=%async_computation.7 | async-start | bytes 1310720 | tf_op jit(solution)/shard_map/all_gather | solution.py:83
Sparse Core Ops, SparseCore 0:
  122.6 23.1 reduce-scatter.2
  147.7 16.7 all-gather.2
  170.5 24.8 reduce-scatter.4
  197.4 16.7 all-gather.4
where the time goes:
time: 224 us; the launch traced here: 223 us
  blocking collectives  92.4 us (41%)
  waiting for transfers between devices  77 us (34%)
  between operations  13.9 us (6%)
  starting transfers between devices  12.7 us (6%)
  other arithmetic  9.96 us (4%)
  matrix products  9.85 us (4%)
  local copies, waits for them, and re-layouts  7.14 us (3%)
    psum x1, blocking collectives, per_device(): mean = lax.psum(jnp.sum(proj, axis=0), ('dp', 'cent')) / total_rows  40.8 us
    psum x1, blocking collectives, per_device(): lax.psum(jnp.sum((proj - mean) ** 2, axis=0), ('dp', 'cent')) / total_rows  40 us
    reduce_scatter x2, waiting for transfers between devices, per_device(): lax.psum_scatter(num, 'dp', scatter_dimension=0, tiled=True)  35.3 us
    all_gather x2, waiting for transfers between devices, per_device(): current = lax.all_gather(fresh, 'dp', axis=0, tiled=True)  33.7 us
    unnamed x2, blocking collectives  11.6 us
    all_to_all x1, waiting for transfers between devices, per_device(): lax.all_to_all(packed.reshape(group_count, capacity, width), 'cent', spli...  7.92 us
    all_to_all x1, starting transfers between devices, per_device(): lax.all_to_all(filled.reshape(group_count, capacity), 'cent', split_axis=...  7.25 us
    all_to_all x1, starting transfers between devices, per_device(): lax.all_to_all(packed.reshape(group_count, capacity, width), 'cent', spli...  5.31 us
  transfers between devices with their start and end apart: 6, of which 5 were waited for; matrix products, arithmetic and copies ran while one was open for 4% of the time, Pallas kernels for 0%

commit v1 on v0

v1 whole, which is shorter than its diff:
```python
import functools

import jax
import jax.numpy as jnp
from jax import lax
from jax.experimental import pallas as pl
from jax.experimental.pallas import tpu as pltpu
from jax.sharding import PartitionSpec as P

STEPS = 2
CORES = 2

beta_scale = 0.0625
prior_weight = 1.0
eps_value = 1e-05
LOG2E = 1.4426950408889634
DEAD = 1024.0
UNROLL = 8
TILE = 256

MESH = pl.DeviceIdType.MESH
NT = (((1,), (1,)), ((), ()))


def loop(n, body):
    if n <= UNROLL:
        for i in range(n):
            body(i)
    else:
        lax.fori_loop(0, n, lambda i, c: (body(i), c)[1], 0)


def kernel(
    n_dp, n_cent, cap, blocks,
    frag_hbm, order_ref, group_ref, w1_hbm, w2_hbm, cent_hbm,
    out_ref,
    frag, w1, w2, cur, proj, packed, rows, expo, live, sm_out, sm_in, st_out, st_dp, st_cent,
    in_sem, a_send, a_recv, y_send, y_recv, c_send, c_recv, s1_send, s1_recv, s2_send, s2_recv,
    sm_send, sm_recv, f_send, f_recv,
):
    dp, ce = lax.axis_index("dp"), lax.axis_index("cent")
    core = lax.rem(dp, CORES)
    n_y = n_dp // CORES
    here_y = dp // CORES
    mate = here_y * CORES + (1 - core)
    rows_here, emb = frag.shape
    hid = w1.shape[1]
    width = w2.shape[1]
    half = cur.shape[0]
    per_block = n_cent // blocks
    plane_rows = n_cent * cap

    def at(d, c):
        return {"dp": d, "cent": c}

    loads = [pltpu.make_async_copy(frag_hbm, frag, in_sem.at[0])]
    n_tiles = hid // TILE
    for j in range(n_tiles):
        cols = pl.ds(j * TILE, TILE)
        loads.append(pltpu.make_async_copy(w1_hbm.at[:, cols], w1.at[:, cols], in_sem.at[1 + j]))
    loads.append(pltpu.make_async_copy(w2_hbm, w2, in_sem.at[1 + n_tiles]))
    loads.append(pltpu.make_async_copy(cent_hbm.at[core], cur, in_sem.at[2 + n_tiles]))
    for c in loads:
        c.start()

    barrier = pltpu.get_barrier_semaphore()

    def greet_dp(k):
        pl.semaphore_signal(barrier, 1, device_id=at(lax.rem(dp + k + 1, n_dp), ce), device_id_type=MESH)

    def greet_cent(k):
        pl.semaphore_signal(barrier, 1, device_id=at(dp, lax.rem(ce + k + 1, n_cent)), device_id_type=MESH)

    loop(n_dp - 1, greet_dp)
    loop(n_cent - 1, greet_cent)

    groups = group_ref[...]
    member = lax.broadcasted_iota(jnp.int32, (max(n_cent, 16), rows_here), 0) == groups
    memberf = member.astype(jnp.float32)
    earlier = (
        lax.broadcasted_iota(jnp.int32, (rows_here, rows_here), 0)
        < lax.broadcasted_iota(jnp.int32, (rows_here, rows_here), 1)
    ).astype(jnp.float32).astype(jnp.bfloat16)
    counts = jnp.dot(memberf.astype(jnp.bfloat16), earlier, preferred_element_type=jnp.float32)
    rank = jnp.sum(counts * memberf, axis=0, keepdims=True).astype(jnp.int32)
    slot = groups * cap + rank
    place = (
        lax.broadcasted_iota(jnp.int32, (plane_rows, rows_here), 0) == slot
    ).astype(jnp.float32).astype(jnp.bfloat16)
    taken = (
        lax.broadcasted_iota(jnp.int32, (rows_here, rows_here), 0) == order_ref[...]
    ).astype(jnp.float32).astype(jnp.bfloat16)
    pickf = lax.dot_general(place, taken, NT, preferred_element_type=jnp.float32)
    pick = pickf.astype(jnp.bfloat16)
    dead = DEAD * (1.0 - jnp.sum(pickf, axis=1, keepdims=True))
    mark = jnp.where(
        lax.broadcasted_iota(jnp.int32, (plane_rows, width), 1) == 0, dead, 0.0
    )

    loads[0].wait()
    loads[1 + n_tiles].wait()
    for j in range(n_tiles):
        loads[1 + j].wait()
        h = jnp.dot(frag[...], w1[:, j * TILE:(j + 1) * TILE], preferred_element_type=jnp.float32)
        h = jax.nn.gelu(h, approximate=True).astype(jnp.bfloat16)
        p = jnp.dot(h, w2[j * TILE:(j + 1) * TILE, :], preferred_element_type=jnp.float32)
        if j == 0:
            proj[...] = p
        else:
            proj[...] += p

    pr = proj[...]
    mean = jnp.sum(pr, axis=0, keepdims=True) / rows_here
    square = jnp.sum((pr - mean) ** 2, axis=0, keepdims=True)
    st_out[0, 0:1, :] = mean
    st_out[0, 1:2, :] = square
    st_dp[dp, 0:1, :] = mean
    st_dp[dp, 1:2, :] = square

    pl.semaphore_wait(barrier, n_dp - 1 + n_cent - 1)

    def dp_copy(k):
        return pltpu.make_async_remote_copy(
            st_out.at[0], st_dp.at[dp], s1_send.at[k], s1_recv.at[k],
            device_id=at(lax.rem(dp + k + 1, n_dp), ce), device_id_type=MESH)

    def cent_copy(k):
        return pltpu.make_async_remote_copy(
            st_out.at[1], st_cent.at[ce], s2_send.at[k], s2_recv.at[k],
            device_id=at(dp, lax.rem(ce + k + 1, n_cent)), device_id_type=MESH)

    def combine(buffer, count, each):
        got = buffer[...]
        means, squares = got[:, 0, :], got[:, 1, :]
        mean = jnp.sum(means, axis=0, keepdims=True) / count
        square = jnp.sum(squares, axis=0, keepdims=True) + each * jnp.sum(
            (means - mean) ** 2, axis=0, keepdims=True)
        return mean, square

    loop(n_dp - 1, lambda k: dp_copy(k).start())
    loop(n_dp - 1, lambda k: dp_copy(k).wait_recv())
    mean, square = combine(st_dp, n_dp, float(rows_here))
    st_out[1, 0:1, :] = mean
    st_out[1, 1:2, :] = square
    st_cent[ce, 0:1, :] = mean
    st_cent[ce, 1:2, :] = square
    loop(n_cent - 1, lambda k: cent_copy(k).start())
    loop(n_cent - 1, lambda k: cent_copy(k).wait_recv())
    mean, square = combine(st_cent, n_cent, float(rows_here * n_dp))
    var = square / float(rows_here * n_dp * n_cent)
    z = ((proj[...] - mean) * lax.rsqrt(var + eps_value)).astype(jnp.bfloat16)
    full = jnp.dot(pick, z, preferred_element_type=jnp.float32) + mark
    packed[...] = full.astype(jnp.bfloat16).reshape(n_cent, cap, width)

    def a_copy(k):
        peer = lax.rem(ce + k + 1, n_cent)
        return pltpu.make_async_remote_copy(
            packed.at[peer], rows.at[dp, ce], a_send.at[peer], a_recv.at[ce],
            device_id=at(dp, peer), device_id_type=MESH)

    def a_arrival(src):
        return pltpu.make_async_copy(packed.at[src], rows.at[dp, src], a_recv.at[src])

    a_arrival(ce).start()
    loop(n_cent - 1, lambda k: a_copy(k).start())

    def part(plane, b):
        return rows.at[plane, pl.ds(b * per_block, per_block)]

    def y_copy(k, b):
        return pltpu.make_async_remote_copy(
            part(dp, b), part(dp, b), y_send.at[k, b], y_recv.at[k, b],
            device_id=at(lax.rem(here_y + k, n_y) * CORES + core, ce), device_id_type=MESH)

    def plane_of(k, which):
        return lax.rem(here_y + n_y - k, n_y) * CORES + which

    def y_arrival(k, b):
        plane = plane_of(k, core)
        return pltpu.make_async_copy(part(plane, b), part(plane, b), y_recv.at[k, b])

    def c_copy(k, b):
        plane = plane_of(k, core)
        return pltpu.make_async_remote_copy(
            part(plane, b), part(plane, b), c_send.at[k, b], c_recv.at[k, b],
            device_id=at(mate, ce), device_id_type=MESH)

    mine = ce // per_block
    for i in range(blocks):
        b = lax.rem(mine + blocks - i, blocks)
        loop(per_block, lambda q: a_arrival(b * per_block + q).wait())
        for k in range(1, n_y):
            y_copy(k, b).start()
        c_copy(0, b).start()

    loads[2 + n_tiles].wait()
    selector = (
        (lax.broadcasted_iota(jnp.int32, (16, width), 0) == 0)
        & (lax.broadcasted_iota(jnp.int32, (16, width), 1) == 0)
    ).astype(jnp.float32).astype(jnp.bfloat16)

    def sm_copy(step, plane):
        return pltpu.make_async_remote_copy(
            sm_out.at[step, plane], sm_in.at[step, plane],
            sm_send.at[step, plane], sm_recv.at[step, plane],
            device_id=at(mate, ce), device_id_type=MESH)

    n_sub = plane_rows // TILE
    sub_cents = TILE // cap

    def sub_rows(plane, t):
        return rows[plane, t * sub_cents:(t + 1) * sub_cents].reshape(TILE, width)

    def first_pass(step, plane, rounded, cnorm):
        for t in range(n_sub):
            lanes = slice(t * TILE, (t + 1) * TILE)
            x = sub_rows(plane, t)
            if step == 0:
                flag = lax.dot_general(selector, x, NT, preferred_element_type=jnp.float32)
                live[plane, :, lanes] = (flag[0:1] < 0.5 * DEAD).astype(jnp.float32)
            s = lax.dot_general(rounded, x, NT, preferred_element_type=jnp.float32)
            s = s * (2.0 * beta_scale * LOG2E) - cnorm
            top = jnp.max(s, axis=0, keepdims=True)
            e = jnp.exp2(s - top)
            expo[plane, :, lanes] = e
            sm_out[step, plane, 0:1, lanes] = top
            sm_out[step, plane, 1:2, lanes] = jnp.sum(e, axis=0, keepdims=True)
        sm_copy(step, plane).start()

    def second_pass(step, plane, first, num, den):
        sm_copy(step, plane).wait_recv()
        for t in range(n_sub):
            lanes = slice(t * TILE, (t + 1) * TILE)
            m0, s0 = sm_out[step, plane, 0:1, lanes], sm_out[step, plane, 1:2, lanes]
            m1, s1 = sm_in[step, plane, 0:1, lanes], sm_in[step, plane, 1:2, lanes]
            top = jnp.maximum(m0, m1)
            own = jnp.exp2(m0 - top)
            total = s0 * own + s1 * jnp.exp2(m1 - top)
            r = (expo[plane, :, lanes] * (own / total * live[plane, :, lanes])).astype(jnp.bfloat16)
            num = num + jnp.dot(r, sub_rows(plane, t), preferred_element_type=jnp.float32)
            den = den + jnp.sum(r.astype(jnp.float32), axis=1, keepdims=True)
        return num, den

    def all_planes(body, carry):
        if n_dp <= UNROLL:
            for k in range(n_y):
                for other in range(CORES):
                    carry = body(plane_of(k, core if other == 0 else 1 - core), carry)
            return carry
        return lax.fori_loop(
            0, n_dp, lambda i, c: body(plane_of(i // CORES, lax.rem(core + i, CORES)), c), carry)

    for step in range(STEPS):
        current = cur[...]
        rounded = current.astype(jnp.bfloat16)
        cnorm = (beta_scale * LOG2E) * jnp.sum(current * current, axis=1, keepdims=True)
        if step == 0:
            first_pass(step, plane_of(0, core), rounded, cnorm)
            for i in range(blocks):
                c_copy(0, lax.rem(mine + blocks - i, blocks)).wait_recv()
            first_pass(step, plane_of(0, 1 - core), rounded, cnorm)
            for k in range(1, n_y):
                for i in range(blocks):
                    b = lax.rem(mine + blocks - i, blocks)
                    y_arrival(k, b).wait()
                    c_copy(k, b).start()
                first_pass(step, plane_of(k, core), rounded, cnorm)
                for i in range(blocks):
                    c_copy(k, lax.rem(mine + blocks - i, blocks)).wait_recv()
                first_pass(step, plane_of(k, 1 - core), rounded, cnorm)
        else:
            all_planes(lambda plane, c: (first_pass(step, plane, rounded, cnorm), c)[1], 0)
        num = jnp.zeros((half, width), jnp.float32)
        den = jnp.zeros((half, 1), jnp.float32)
        num, den = all_planes(
            lambda plane, c: second_pass(step, plane, False, c[0], c[1]), (num, den))
        fresh = (num + prior_weight * cur[...]) / (den + prior_weight)
        if step < STEPS - 1:
            cur[...] = fresh
        else:
            out_ref[core] = fresh

    final = pltpu.make_async_remote_copy(
        out_ref.at[core], out_ref.at[core], f_send, f_recv,
        device_id=at(mate, ce), device_id_type=MESH)
    final.start()
    loop(n_dp - 1, lambda k: dp_copy(k).wait_send())
    loop(n_cent - 1, lambda k: cent_copy(k).wait_send())
    loop(n_cent - 1, lambda k: a_copy(k).wait_send())
    for k in range(n_y):
        for b in range(blocks):
            if k:
                y_copy(k, b).wait_send()
            c_copy(k, b).wait_send()
    for step in range(STEPS):
        loop(n_dp, lambda plane: sm_copy(step, plane).wait_send())
    final.wait()


def per_device(fragments, order, group_ids, w_first, w_second, centroids):
    rows_here, emb = fragments.shape
    hid, width = w_second.shape
    n_dp, n_cent = lax.axis_size("dp"), lax.axis_size("cent")
    n_y = n_dp // CORES
    cap = max(16, 2 * rows_here // n_cent)
    plane_rows = n_cent * cap
    blocks = min(n_cent, 8)
    half = centroids.shape[0] // CORES
    n_tiles = hid // TILE
    f32, bf16 = jnp.float32, jnp.bfloat16
    dma = pltpu.SemaphoreType.DMA
    vmem = pl.BlockSpec(memory_space=pltpu.VMEM)
    anyspace = pl.BlockSpec(memory_space=pl.ANY)
    need = 2 * (emb * hid + rows_here * emb + n_dp * plane_rows * width) + 4 * n_dp * plane_rows * half
    out = pl.pallas_call(
        functools.partial(kernel, n_dp, n_cent, cap, blocks),
        out_shape=jax.ShapeDtypeStruct((CORES, half, width), f32),
        in_specs=[anyspace, vmem, vmem, anyspace, anyspace, anyspace],
        out_specs=vmem,
        scratch_shapes=[
            pltpu.VMEM((rows_here, emb), bf16),
            pltpu.VMEM((emb, hid), bf16),
            pltpu.VMEM((hid, width), bf16),
            pltpu.VMEM((half, width), f32),
            pltpu.VMEM((rows_here, width), f32),
            pltpu.VMEM((n_cent, cap, width), bf16),
            pltpu.VMEM((n_dp, n_cent, cap, width), bf16),
            pltpu.VMEM((n_dp, half, plane_rows), f32),
            pltpu.VMEM((n_dp, 1, plane_rows), f32),
            pltpu.VMEM((STEPS, n_dp, 2, plane_rows), f32),
            pltpu.VMEM((STEPS, n_dp, 2, plane_rows), f32),
            pltpu.VMEM((2, 2, width), f32),
            pltpu.VMEM((n_dp, 2, width), f32),
            pltpu.VMEM((n_cent, 2, width), f32),
            dma((3 + n_tiles,)),
            dma((n_cent,)), dma((n_cent,)),
            dma((n_y, blocks)), dma((n_y, blocks)),
            dma((n_y, blocks)), dma((n_y, blocks)),
            dma((n_dp,)), dma((n_dp,)),
            dma((n_cent,)), dma((n_cent,)),
            dma((STEPS, n_dp)), dma((STEPS, n_dp)),
            dma, dma,
        ],
        compiler_params=pltpu.CompilerParams(
            collective_id=0, has_side_effects=True, vmem_limit_bytes=min(58 << 20, need + (14 << 20))
        ),
    )(
        fragments, order, group_ids.reshape(1, rows_here), w_first, w_second,
        centroids.reshape(CORES, half, width),
    )
    return out.reshape(CORES * half, width)


def solution(mesh):
    return jax.shard_map(
        per_device,
        mesh=mesh,
        in_specs=(
            P(("dp", "cent"), None),
            P(("dp", "cent"), None),
            P(("dp", "cent"), None),
            P(),
            P(),
            P("cent", None),
        ),
        out_specs=P("cent", None),
        check_vma=False,
    )
```

time: 224 us -> 41.4 us (0.18)
  blocking collectives: 92.4 us -> 0 us
  waiting for transfers between devices: 77 us -> 0 us
  Pallas kernels: 0 us -> 33.8 us
  between operations: 13.9 us -> 0.02 us
  starting transfers between devices: 12.7 us -> 0 us
  other arithmetic: 9.96 us -> 0 us
  matrix products: 9.85 us -> 0 us
    psum x2 -> x0, blocking collectives: 80.9 us -> none  [the longest x1 40.8 us: per_device(): mean = lax.psum(jnp.sum(proj, axis=0), ('dp', 'cent')) / total_rows]
    reduce_scatter x2 -> x0, waiting for transfers between devices: 35.3 us -> none  [per_device(): lax.psum_scatter(num, 'dp', scatter_dimension=0, tiled=True)]
    pallas_call x0 -> x1, Pallas kernels: none -> 33.8 us  [per_device(): pl.pallas_call(functools.partial(kernel, n_dp, n_cent, cap, blocks), out_...]
    all_gather x2 -> x0, waiting for transfers between devices: 33.7 us -> none  [per_device(): current = lax.all_gather(fresh, 'dp', axis=0, tiled=True)]
    all_to_all x2 -> x0, starting transfers between devices: 12.6 us -> none  [the longest x1 7.25 us: per_device(): lax.all_to_all(filled.reshape(group_count, capacity), 'cent', split_axis=...]
    unnamed x2 -> x0, blocking collectives: 11.6 us -> none
    dot_general x7 -> x0, matrix products: 9.85 us -> none  [the longest x2 2.9 us: per_device(): lax.dot_general(resp, received, (((0,), (0,)), ((), ())), preferred_eleme...]
    all_to_all x2 -> x0, waiting for transfers between devices: 7.93 us -> none  [the longest x1 7.92 us: per_device(): lax.all_to_all(packed.reshape(group_count, capacity, width), 'cent', spli...]
  transfers between devices with their start and end apart: 6 -> 0, of which waited for: 5 -> 0; matrix products, arithmetic and copies ran while one was open for 4% -> 0% of each run, Pallas kernels for 0% -> 0%
where the time goes in v1:
time: 41.4 us; the launch traced here: 41.1 us
  Pallas kernels  33.8 us (82%)
  local copies, waits for them, and re-layouts  7.23 us (17%)
    pallas_call x1, Pallas kernels, per_device(): pl.pallas_call(functools.partial(kernel, n_dp, n_cent, cap, blocks), out_...  33.8 us
    unnamed x13, local copies, waits for them, and re-layouts  7.23 us

profile of v1, /device:TPU:0, one launch (start us, length us, event | category | flops | bytes accessed | tf_op | source)
XLA Modules:
  0.0 41.1 jit_solution(12048011580191374035)
XLA Ops:
  0.0 0.0 copy-start
  0.0 1.6 %copy-done = bf16[1024,1024]{1,0:T(8,128)(2,1)S(1)} copy-done((bf16[1024,1024]{1,0:T(8,128)(2,1)S(1)}, bf16[1024,1024]{1,0:T(8,128)(2,1)}, u32[]{:S(2)}) %copy-start) | copy-done | bytes 2097176
  1.6 0.0 copy-start.1
  1.6 1.2 %copy-done.1 = f32[1024,256]{1,0:T(8,128)S(1)} copy-done((f32[1024,256]{1,0:T(8,128)S(1)}, f32[1024,256]{1,0:T(8,128)}, u32[]{:S(2)}) %copy-start.1) | copy-done | bytes 1048600
  2.8 0.0 copy-start.2
  2.8 1.0 %copy-done.2 = bf16[256,1024]{1,0:T(8,128)(2,1)S(1)} copy-done((bf16[256,1024]{1,0:T(8,128)(2,1)S(1)}, bf16[256,1024]{1,0:T(8,128)(2,1)}, u32[]{:S(2)}) %copy-start.2) | copy-done | bytes 524312
  3.9 0.0 copy-start.3
  3.9 1.0 %copy-done.3 = bf16[1024,256]{1,0:T(8,128)(2,1)S(1)} copy-done((bf16[1024,256]{1,0:T(8,128)(2,1)S(1)}, bf16[1024,256]{1,0:T(8,128)(2,1)}, u32[]{:S(2)}) %copy-start.3) | copy-done | bytes 524312
  4.9 0.0 copy-start.4
  4.9 0.7 %copy-done.4 = s32[1,256]{1,0:T(1,128)S(1)} copy-done((s32[1,256]{1,0:T(1,128)S(1)}, s32[1,256]{1,0:T(1,128)}, u32[]{:S(2)}) %copy-start.4) | copy-done | bytes 1048
  5.6 0.0 copy-start.5
  5.6 0.7 %copy-done.5 = s32[256,1]{0,1:T(1,128)S(1)} copy-done((s32[256,1]{0,1:T(1,128)S(1)}, s32[256,1]{0,1:T(1,128)}, u32[]{:S(2)}) %copy-start.5) | copy-done | bytes 1048
  6.3 33.8 %shard_map.64 = f32[2,512,256]{2,1,0:T(8,128)S(1)} custom-call(bf16[256,1024]{1,0:T(8,128)(2,1)S(1)} %copy-done.2, s32[1,256]{1,0:T(1,128)S(1)} %copy-done.4, s32[1,256]{1,0:T(1,128)S(1)} %bitcast.5, bf16[1024,1024]{1,0:T(8,128)(2,1)S(1)} %copy-done, bf16[1024,256]{1,0:T(8,128)(2,1)S(1)} %copy-done.3, f32[2,512,256]{2,1,0:T(8,128)S(1)} %bitcast.4), custom_call_target="tpu_custom_call" | custom-call | tf_op jit(solution)/shard_map/pallas_call | solution.py:315
  40.1 1.0 %copy.8 = f32[1024,256]{1,0:T(8,128)} copy(f32[1024,256]{1,0:T(8,128)S(1)} %bitcast.3) | data formatting | bytes 2097152
Async XLA Ops:
  0.0 1.6 %copy-start = (bf16[1024,1024]{1,0:T(8,128)(2,1)S(1)}, bf16[1024,1024]{1,0:T(8,128)(2,1)}, u32[]{:S(2)}) copy-start(bf16[1024,1024]{1,0:T(8,128)(2,1)} %w1_hbm.1) | copy-start | bytes 6291460
  1.6 1.2 %copy-start.1 = (f32[1024,256]{1,0:T(8,128)S(1)}, f32[1024,256]{1,0:T(8,128)}, u32[]{:S(2)}) copy-start(f32[1024,256]{1,0:T(8,128)} %param.11) | copy-start | bytes 3145732
  2.8 1.0 %copy-start.2 = (bf16[256,1024]{1,0:T(8,128)(2,1)S(1)}, bf16[256,1024]{1,0:T(8,128)(2,1)}, u32[]{:S(2)}) copy-start(bf16[256,1024]{1,0:T(8,128)(2,1)} %frag_hbm.1) | copy-start | bytes 1572868
  3.9 1.0 %copy-start.3 = (bf16[1024,256]{1,0:T(8,128)(2,1)S(1)}, bf16[1024,256]{1,0:T(8,128)(2,1)}, u32[]{:S(2)}) copy-start(bf16[1024,256]{1,0:T(8,128)(2,1)} %w2_hbm.1) | copy-start | bytes 1572868
  4.9 0.7 %copy-start.4 = (s32[1,256]{1,0:T(1,128)S(1)}, s32[1,256]{1,0:T(1,128)}, u32[]{:S(2)}) copy-start(s32[1,256]{1,0:T(1,128)} %order_ref.1) | copy-start | bytes 3076
  5.6 0.7 %copy-start.5 = (s32[256,1]{0,1:T(1,128)S(1)}, s32[256,1]{0,1:T(1,128)}, u32[]{:S(2)}) copy-start(s32[256,1]{0,1:T(1,128)} %param.8) | copy-start | bytes 3076

commit v2 on v1

--- a/solution.py
+++ b/solution.py
@@ -17,6 +17,7 @@
 DEAD = 1024.0
 UNROLL = 8
 TILE = 256
+VMEM_BYTES = 60 << 20
 
 MESH = pl.DeviceIdType.MESH
 NT = (((1,), (1,)), ((), ()))
@@ -32,9 +33,9 @@
 
 def kernel(
     n_dp, n_cent, cap, blocks,
-    frag_hbm, order_ref, group_ref, w1_hbm, w2_hbm, cent_hbm,
+    frag_hbm, order_hbm, group_hbm, w1_hbm, w2_hbm, cent_hbm,
     out_ref,
-    frag, w1, w2, cur, proj, packed, rows, expo, live, sm_out, sm_in, st_out, st_dp, st_cent,
+    frag, order_ref, group_ref, w1, w2, cur, proj, packed, rows, zrows, expo, live, sm_out, sm_in, stats,
     in_sem, a_send, a_recv, y_send, y_recv, c_send, c_recv, s1_send, s1_recv, s2_send, s2_recv,
     sm_send, sm_recv, f_send, f_recv,
 ):
@@ -53,14 +54,18 @@
     def at(d, c):
         return {"dp": d, "cent": c}
 
+    n_tiles = hid // TILE
+    small = [
+        pltpu.make_async_copy(group_hbm, group_ref, in_sem.at[3 + n_tiles]),
+        pltpu.make_async_copy(order_hbm, order_ref, in_sem.at[4 + n_tiles]),
+    ]
     loads = [pltpu.make_async_copy(frag_hbm, frag, in_sem.at[0])]
-    n_tiles = hid // TILE
     for j in range(n_tiles):
         cols = pl.ds(j * TILE, TILE)
         loads.append(pltpu.make_async_copy(w1_hbm.at[:, cols], w1.at[:, cols], in_sem.at[1 + j]))
     loads.append(pltpu.make_async_copy(w2_hbm, w2, in_sem.at[1 + n_tiles]))
     loads.append(pltpu.make_async_copy(cent_hbm.at[core], cur, in_sem.at[2 + n_tiles]))
-    for c in loads:
+    for c in small + loads:
         c.start()
 
     barrier = pltpu.get_barrier_semaphore()
@@ -74,6 +79,8 @@
     loop(n_dp - 1, greet_dp)
     loop(n_cent - 1, greet_cent)
 
+    for c in small:
+        c.wait()
     groups = group_ref[...]
     member = lax.broadcasted_iota(jnp.int32, (max(n_cent, 16), rows_here), 0) == groups
     memberf = member.astype(jnp.float32)
@@ -111,47 +118,28 @@
 
     pr = proj[...]
     mean = jnp.sum(pr, axis=0, keepdims=True) / rows_here
-    square = jnp.sum((pr - mean) ** 2, axis=0, keepdims=True)
-    st_out[0, 0:1, :] = mean
-    st_out[0, 1:2, :] = square
-    st_dp[dp, 0:1, :] = mean
-    st_dp[dp, 1:2, :] = square
-
-    pl.semaphore_wait(barrier, n_dp - 1 + n_cent - 1)
-
-    def dp_copy(k):
-        return pltpu.make_async_remote_copy(
-            st_out.at[0], st_dp.at[dp], s1_send.at[k], s1_recv.at[k],
-            device_id=at(lax.rem(dp + k + 1, n_dp), ce), device_id_type=MESH)
-
-    def cent_copy(k):
-        return pltpu.make_async_remote_copy(
-            st_out.at[1], st_cent.at[ce], s2_send.at[k], s2_recv.at[k],
-            device_id=at(dp, lax.rem(ce + k + 1, n_cent)), device_id_type=MESH)
-
-    def combine(buffer, count, each):
-        got = buffer[...]
-        means, squares = got[:, 0, :], got[:, 1, :]
-        mean = jnp.sum(means, axis=0, keepdims=True) / count
-        square = jnp.sum(squares, axis=0, keepdims=True) + each * jnp.sum(
-            (means - mean) ** 2, axis=0, keepdims=True)
-        return mean, square
-
-    loop(n_dp - 1, lambda k: dp_copy(k).start())
-    loop(n_dp - 1, lambda k: dp_copy(k).wait_recv())
-    mean, square = combine(st_dp, n_dp, float(rows_here))
-    st_out[1, 0:1, :] = mean
-    st_out[1, 1:2, :] = square
-    st_cent[ce, 0:1, :] = mean
-    st_cent[ce, 1:2, :] = square
-    loop(n_cent - 1, lambda k: cent_copy(k).start())
-    loop(n_cent - 1, lambda k: cent_copy(k).wait_recv())
-    mean, square = combine(st_cent, n_cent, float(rows_here * n_dp))
-    var = square / float(rows_here * n_dp * n_cent)
-    z = ((proj[...] - mean) * lax.rsqrt(var + eps_value)).astype(jnp.bfloat16)
+    centered = pr - mean
+    square = jnp.sum(centered * centered, axis=0, keepdims=True)
+    stats[ce, dp, 0:1, :] = mean
+    stats[ce, dp, 1:2, :] = square
+    z = (centered * lax.rsqrt(square / rows_here + eps_value)).astype(jnp.bfloat16)
     full = jnp.dot(pick, z, preferred_element_type=jnp.float32) + mark
     packed[...] = full.astype(jnp.bfloat16).reshape(n_cent, cap, width)
 
+    pl.semaphore_wait(barrier, n_dp - 1 + n_cent - 1)
+
+    def dp_copy(k):
+        return pltpu.make_async_remote_copy(
+            stats.at[ce, dp], stats.at[ce, dp], s1_send.at[k], s1_recv.at[k],
+            device_id=at(lax.rem(dp + k + 1, n_dp), ce), device_id_type=MESH)
+
+    def cent_copy(k):
+        return pltpu.make_async_remote_copy(
+            stats.at[ce], stats.at[ce], s2_send.at[k], s2_recv.at[k],
+            device_id=at(dp, lax.rem(ce + k + 1, n_cent)), device_id_type=MESH)
+
+    loop(n_dp - 1, lambda k: dp_copy(k).start())
+
     def a_copy(k):
         peer = lax.rem(ce + k + 1, n_cent)
         return pltpu.make_async_remote_copy(
@@ -163,6 +151,8 @@
 
     a_arrival(ce).start()
     loop(n_cent - 1, lambda k: a_copy(k).start())
+    loop(n_dp - 1, lambda k: dp_copy(k).wait_recv())
+    loop(n_cent - 1, lambda k: cent_copy(k).start())
 
     def part(plane, b):
         return rows.at[plane, pl.ds(b * per_block, per_block)]
@@ -193,6 +183,14 @@
             y_copy(k, b).start()
         c_copy(0, b).start()
 
+    loop(n_cent - 1, lambda k: cent_copy(k).wait_recv())
+    got = stats[...]
+    total = jnp.sum(got, axis=(0, 1))
+    mean = total[0:1] / (n_dp * n_cent)
+    apart = jnp.sum((got - mean) ** 2, axis=(0, 1))
+    var = (total[1:2] + rows_here * apart[0:1]) / float(rows_here * n_dp * n_cent)
+    inverse = lax.rsqrt(var + eps_value)
+
     loads[2 + n_tiles].wait()
     selector = (
         (lax.broadcasted_iota(jnp.int32, (16, width), 0) == 0)
@@ -209,15 +207,26 @@
     sub_cents = TILE // cap
 
     def sub_rows(plane, t):
-        return rows[plane, t * sub_cents:(t + 1) * sub_cents].reshape(TILE, width)
+        return zrows[plane, t * TILE:(t + 1) * TILE]
+
+    def normalise(plane, t):
+        part = slice(t * sub_cents, (t + 1) * sub_cents)
+        raw = rows[plane, part]
+        own = stats[part, plane]
+        scale = jnp.sqrt(own[:, 1:2] / rows_here + eps_value) * inverse
+        shift = (own[:, 0:1] - mean) * inverse
+        x = (raw.astype(jnp.float32) * scale + shift).astype(jnp.bfloat16)
+        zrows[plane, t * TILE:(t + 1) * TILE] = x.reshape(TILE, width)
+        flag = lax.dot_general(
+            selector, raw.reshape(TILE, width), NT, preferred_element_type=jnp.float32)
+        live[plane, :, t * TILE:(t + 1) * TILE] = (flag[0:1] < 0.5 * DEAD).astype(jnp.float32)
 
     def first_pass(step, plane, rounded, cnorm):
         for t in range(n_sub):
             lanes = slice(t * TILE, (t + 1) * TILE)
+            if step == 0:
+                normalise(plane, t)
             x = sub_rows(plane, t)
-            if step == 0:
-                flag = lax.dot_general(selector, x, NT, preferred_element_type=jnp.float32)
-                live[plane, :, lanes] = (flag[0:1] < 0.5 * DEAD).astype(jnp.float32)
             s = lax.dot_general(rounded, x, NT, preferred_element_type=jnp.float32)
             s = s * (2.0 * beta_scale * LOG2E) - cnorm
             top = jnp.max(s, axis=0, keepdims=True)
@@ -310,29 +319,29 @@
     f32, bf16 = jnp.float32, jnp.bfloat16
     dma = pltpu.SemaphoreType.DMA
     vmem = pl.BlockSpec(memory_space=pltpu.VMEM)
-    anyspace = pl.BlockSpec(memory_space=pl.ANY)
-    need = 2 * (emb * hid + rows_here * emb + n_dp * plane_rows * width) + 4 * n_dp * plane_rows * half
+    hbm = pl.BlockSpec(memory_space=pltpu.HBM)
     out = pl.pallas_call(
         functools.partial(kernel, n_dp, n_cent, cap, blocks),
         out_shape=jax.ShapeDtypeStruct((CORES, half, width), f32),
-        in_specs=[anyspace, vmem, vmem, anyspace, anyspace, anyspace],
+        in_specs=[hbm] * 6,
         out_specs=vmem,
         scratch_shapes=[
             pltpu.VMEM((rows_here, emb), bf16),
+            pltpu.VMEM((1, rows_here), jnp.int32),
+            pltpu.VMEM((1, rows_here), jnp.int32),
             pltpu.VMEM((emb, hid), bf16),
             pltpu.VMEM((hid, width), bf16),
             pltpu.VMEM((half, width), f32),
             pltpu.VMEM((rows_here, width), f32),
             pltpu.VMEM((n_cent, cap, width), bf16),
             pltpu.VMEM((n_dp, n_cent, cap, width), bf16),
+            pltpu.VMEM((n_dp, plane_rows, width), bf16),
             pltpu.VMEM((n_dp, half, plane_rows), f32),
             pltpu.VMEM((n_dp, 1, plane_rows), f32),
             pltpu.VMEM((STEPS, n_dp, 2, plane_rows), f32),
             pltpu.VMEM((STEPS, n_dp, 2, plane_rows), f32),
-            pltpu.VMEM((2, 2, width), f32),
-            pltpu.VMEM((n_dp, 2, width), f32),
-            pltpu.VMEM((n_cent, 2, width), f32),
-            dma((3 + n_tiles,)),
+            pltpu.VMEM((n_cent, n_dp, 2, width), f32),
+            dma((5 + n_tiles,)),
             dma((n_cent,)), dma((n_cent,)),
             dma((n_y, blocks)), dma((n_y, blocks)),
             dma((n_y, blocks)), dma((n_y, blocks)),
@@ -342,7 +351,7 @@
             dma, dma,
         ],
         compiler_params=pltpu.CompilerParams(
-            collective_id=0, has_side_effects=True, vmem_limit_bytes=min(58 << 20, need + (14 << 20))
+            collective_id=0, has_side_effects=True, vmem_limit_bytes=VMEM_BYTES
         ),
     )(
         fragments, order, group_ids.reshape(1, rows_here), w_first, w_second,

time: 41.4 us -> 32.2 us (0.78)
  local copies, waits for them, and re-layouts: 7.23 us -> 2.26 us
  Pallas kernels: 33.8 us -> 29.8 us
    unnamed x13 -> x1, local copies, waits for them, and re-layouts: 7.23 us -> 2.26 us
    pallas_call x1, Pallas kernels: 33.8 us -> 29.8 us  [per_device(): pl.pallas_call(functools.partial(kernel, n_dp, n_cent, cap, blocks), out_...]
where the time goes in v2:
time: 32.2 us; the launch traced here: 32 us
  Pallas kernels  29.8 us (93%)
  local copies, waits for them, and re-layouts  2.26 us (7%)
    pallas_call x1, Pallas kernels, per_device(): pl.pallas_call(functools.partial(kernel, n_dp, n_cent, cap, blocks), out_...  29.8 us
    unnamed x1, local copies, waits for them, and re-layouts  2.26 us

profile of v2, /device:TPU:0, one launch (start us, length us, event | category | flops | bytes accessed | tf_op | source)
XLA Modules:
  0.0 32.0 jit_solution(12262113448864097038)
XLA Ops:
  0.0 29.8 %shard_map.64 = f32[2,512,256]{2,1,0:T(8,128)} custom-call(bf16[256,1024]{1,0:T(8,128)(2,1)} %frag_hbm.1, s32[1,256]{1,0:T(1,128)} %order_hbm.1, s32[1,256]{1,0:T(1,128)} %bitcast.5, bf16[1024,1024]{1,0:T(8,128)(2,1)} %w1_hbm.1, bf16[1024,256]{1,0:T(8,128)(2,1)} %w2_hbm.1, f32[2,512,256]{2,1,0:T(8,128)} %bitcast.4), custom_call_target="tpu_custom_call" | custom-call | tf_op jit(solution)/shard_map/pallas_call | solution.py:323
  29.8 2.3 %copy.8 = f32[1024,256]{1,0:T(8,128)} copy(f32[1024,256]{1,0:T(8,128)} %bitcast.3) | data formatting | bytes 2097152

commit v3 on v2

--- a/solution.py
+++ b/solution.py
@@ -17,6 +17,7 @@
 DEAD = 1024.0
 UNROLL = 8
 TILE = 256
+FINAL = 2
 VMEM_BYTES = 60 << 20
 
 MESH = pl.DeviceIdType.MESH
@@ -31,13 +32,17 @@
         lax.fori_loop(0, n, lambda i, c: (body(i), c)[1], 0)
 
 
+def offsets(n_dp, n_cent):
+    return [(a, b) for b in range(n_cent) for a in range(n_dp) if a or b]
+
+
 def kernel(
     n_dp, n_cent, cap, blocks,
     frag_hbm, order_hbm, group_hbm, w1_hbm, w2_hbm, cent_hbm,
     out_ref,
     frag, order_ref, group_ref, w1, w2, cur, proj, packed, rows, zrows, expo, live, sm_out, sm_in, stats,
     in_sem, a_send, a_recv, y_send, y_recv, c_send, c_recv, s1_send, s1_recv, s2_send, s2_recv,
-    sm_send, sm_recv, f_send, f_recv,
+    sm_send, sm_recv, f_send, f_recv, k_sem,
 ):
     dp, ce = lax.axis_index("dp"), lax.axis_index("cent")
     core = lax.rem(dp, CORES)
@@ -76,8 +81,17 @@
     def greet_cent(k):
         pl.semaphore_signal(barrier, 1, device_id=at(dp, lax.rem(ce + k + 1, n_cent)), device_id_type=MESH)
 
-    loop(n_dp - 1, greet_dp)
-    loop(n_cent - 1, greet_cent)
+    direct = s1_send.shape[0] == n_dp * n_cent
+    if direct:
+        greeted = n_dp * n_cent - 1
+        for a, b in offsets(n_dp, n_cent):
+            pl.semaphore_signal(
+                barrier, 1, device_id=at(lax.rem(dp + a, n_dp), lax.rem(ce + b, n_cent)),
+                device_id_type=MESH)
+    else:
+        greeted = n_dp - 1 + n_cent - 1
+        loop(n_dp - 1, greet_dp)
+        loop(n_cent - 1, greet_cent)
 
     for c in small:
         c.wait()
@@ -126,7 +140,7 @@
     full = jnp.dot(pick, z, preferred_element_type=jnp.float32) + mark
     packed[...] = full.astype(jnp.bfloat16).reshape(n_cent, cap, width)
 
-    pl.semaphore_wait(barrier, n_dp - 1 + n_cent - 1)
+    pl.semaphore_wait(barrier, greeted)
 
     def dp_copy(k):
         return pltpu.make_async_remote_copy(
@@ -138,7 +152,11 @@
             stats.at[ce], stats.at[ce], s2_send.at[k], s2_recv.at[k],
             device_id=at(dp, lax.rem(ce + k + 1, n_cent)), device_id_type=MESH)
 
-    loop(n_dp - 1, lambda k: dp_copy(k).start())
+    def all_copy(a, b):
+        return pltpu.make_async_remote_copy(
+            stats.at[ce, dp], stats.at[ce, dp], s1_send.at[a * n_cent + b], s1_recv.at[a * n_cent + b],
+            device_id=at(lax.rem(dp + a, n_dp), lax.rem(ce + b, n_cent)), device_id_type=MESH)
+
 
     def a_copy(k):
         peer = lax.rem(ce + k + 1, n_cent)
@@ -151,8 +169,10 @@
 
     a_arrival(ce).start()
     loop(n_cent - 1, lambda k: a_copy(k).start())
-    loop(n_dp - 1, lambda k: dp_copy(k).wait_recv())
-    loop(n_cent - 1, lambda k: cent_copy(k).start())
+    if not direct:
+        loop(n_dp - 1, lambda k: dp_copy(k).start())
+        loop(n_dp - 1, lambda k: dp_copy(k).wait_recv())
+        loop(n_cent - 1, lambda k: cent_copy(k).start())
 
     def part(plane, b):
         return rows.at[plane, pl.ds(b * per_block, per_block)]
@@ -182,8 +202,15 @@
         for k in range(1, n_y):
             y_copy(k, b).start()
         c_copy(0, b).start()
-
-    loop(n_cent - 1, lambda k: cent_copy(k).wait_recv())
+        if i == 0 and direct:
+            for far in offsets(n_dp, n_cent):
+                all_copy(*far).start()
+
+    if direct:
+        for far in offsets(n_dp, n_cent):
+            all_copy(*far).wait_recv()
+    else:
+        loop(n_cent - 1, lambda k: cent_copy(k).wait_recv())
     got = stats[...]
     total = jnp.sum(got, axis=(0, 1))
     mean = total[0:1] / (n_dp * n_cent)
@@ -236,8 +263,9 @@
             sm_out[step, plane, 1:2, lanes] = jnp.sum(e, axis=0, keepdims=True)
         sm_copy(step, plane).start()
 
-    def second_pass(step, plane, first, num, den):
-        sm_copy(step, plane).wait_recv()
+    def second_pass(step, plane, h, count, num, den):
+        if h == 0:
+            sm_copy(step, plane).wait_recv()
         for t in range(n_sub):
             lanes = slice(t * TILE, (t + 1) * TILE)
             m0, s0 = sm_out[step, plane, 0:1, lanes], sm_out[step, plane, 1:2, lanes]
@@ -245,7 +273,7 @@
             top = jnp.maximum(m0, m1)
             own = jnp.exp2(m0 - top)
             total = s0 * own + s1 * jnp.exp2(m1 - top)
-            r = (expo[plane, :, lanes] * (own / total * live[plane, :, lanes])).astype(jnp.bfloat16)
+            r = (expo[plane, h * count:(h + 1) * count, lanes] * (own / total * live[plane, :, lanes])).astype(jnp.bfloat16)
             num = num + jnp.dot(r, sub_rows(plane, t), preferred_element_type=jnp.float32)
             den = den + jnp.sum(r.astype(jnp.float32), axis=1, keepdims=True)
         return num, den
@@ -258,6 +286,16 @@
             return carry
         return lax.fori_loop(
             0, n_dp, lambda i, c: body(plane_of(i // CORES, lax.rem(core + i, CORES)), c), carry)
+
+    def final_copy(h):
+        span = pl.ds(h * (half // FINAL), half // FINAL)
+        return pltpu.make_async_remote_copy(
+            cur.at[span], out_ref.at[core, span], f_send.at[h], f_recv.at[h],
+            device_id=at(mate, ce), device_id_type=MESH)
+
+    def keep_copy(h):
+        span = pl.ds(h * (half // FINAL), half // FINAL)
+        return pltpu.make_async_copy(cur.at[span], out_ref.at[core, span], k_sem.at[h])
 
     for step in range(STEPS):
         current = cur[...]
@@ -279,22 +317,25 @@
                 first_pass(step, plane_of(k, 1 - core), rounded, cnorm)
         else:
             all_planes(lambda plane, c: (first_pass(step, plane, rounded, cnorm), c)[1], 0)
-        num = jnp.zeros((half, width), jnp.float32)
-        den = jnp.zeros((half, 1), jnp.float32)
-        num, den = all_planes(
-            lambda plane, c: second_pass(step, plane, False, c[0], c[1]), (num, den))
-        fresh = (num + prior_weight * cur[...]) / (den + prior_weight)
-        if step < STEPS - 1:
-            cur[...] = fresh
-        else:
-            out_ref[core] = fresh
-
-    final = pltpu.make_async_remote_copy(
-        out_ref.at[core], out_ref.at[core], f_send, f_recv,
-        device_id=at(mate, ce), device_id_type=MESH)
-    final.start()
-    loop(n_dp - 1, lambda k: dp_copy(k).wait_send())
-    loop(n_cent - 1, lambda k: cent_copy(k).wait_send())
+        pieces = FINAL if step == STEPS - 1 else 1
+        count = half // pieces
+        for h in range(pieces):
+            num = jnp.zeros((count, width), jnp.float32)
+            den = jnp.zeros((count, 1), jnp.float32)
+            num, den = all_planes(
+                lambda plane, c: second_pass(step, plane, h, count, c[0], c[1]), (num, den))
+            mine_now = slice(h * count, (h + 1) * count)
+            cur[mine_now] = (num + prior_weight * cur[mine_now]) / (den + prior_weight)
+            if step == STEPS - 1:
+                final_copy(h).start()
+                keep_copy(h).start()
+
+    if direct:
+        for far in offsets(n_dp, n_cent):
+            all_copy(*far).wait_send()
+    else:
+        loop(n_dp - 1, lambda k: dp_copy(k).wait_send())
+        loop(n_cent - 1, lambda k: cent_copy(k).wait_send())
     loop(n_cent - 1, lambda k: a_copy(k).wait_send())
     for k in range(n_y):
         for b in range(blocks):
@@ -303,7 +344,9 @@
             c_copy(k, b).wait_send()
     for step in range(STEPS):
         loop(n_dp, lambda plane: sm_copy(step, plane).wait_send())
-    final.wait()
+    for h in range(FINAL):
+        keep_copy(h).wait()
+        final_copy(h).wait()
 
 
 def per_device(fragments, order, group_ids, w_first, w_second, centroids):
@@ -316,15 +359,15 @@
     blocks = min(n_cent, 8)
     half = centroids.shape[0] // CORES
     n_tiles = hid // TILE
+    n_stat = n_dp * n_cent if n_dp * n_cent <= 32 else n_dp
     f32, bf16 = jnp.float32, jnp.bfloat16
     dma = pltpu.SemaphoreType.DMA
-    vmem = pl.BlockSpec(memory_space=pltpu.VMEM)
     hbm = pl.BlockSpec(memory_space=pltpu.HBM)
     out = pl.pallas_call(
         functools.partial(kernel, n_dp, n_cent, cap, blocks),
         out_shape=jax.ShapeDtypeStruct((CORES, half, width), f32),
         in_specs=[hbm] * 6,
-        out_specs=vmem,
+        out_specs=hbm,
         scratch_shapes=[
             pltpu.VMEM((rows_here, emb), bf16),
             pltpu.VMEM((1, rows_here), jnp.int32),
@@ -345,10 +388,10 @@
             dma((n_cent,)), dma((n_cent,)),
             dma((n_y, blocks)), dma((n_y, blocks)),
             dma((n_y, blocks)), dma((n_y, blocks)),
-            dma((n_dp,)), dma((n_dp,)),
+            dma((n_stat,)), dma((n_stat,)),
             dma((n_cent,)), dma((n_cent,)),
             dma((STEPS, n_dp)), dma((STEPS, n_dp)),
-            dma, dma,
+            dma((FINAL,)), dma((FINAL,)), dma((FINAL,)),
         ],
         compiler_params=pltpu.CompilerParams(
             collective_id=0, has_side_effects=True, vmem_limit_bytes=VMEM_BYTES

time: 32.2 us -> 32.6 us (1.012)
  Pallas kernels: 29.8 us -> 30.2 us
    pallas_call x1, Pallas kernels: 29.8 us -> 30.2 us  [per_device(): pl.pallas_call(functools.partial(kernel, n_dp, n_cent, cap, blocks), out_...]
where the time goes in v3:
time: 32.6 us; the launch traced here: 32.4 us
  Pallas kernels  30.2 us (93%)
  local copies, waits for them, and re-layouts  2.26 us (7%)
    pallas_call x1, Pallas kernels, per_device(): pl.pallas_call(functools.partial(kernel, n_dp, n_cent, cap, blocks), out_...  30.2 us
    unnamed x1, local copies, waits for them, and re-layouts  2.26 us

profile of v3, /device:TPU:0, one launch (start us, length us, event | category | flops | bytes accessed | tf_op | source)
XLA Modules:
  0.0 32.4 jit_solution(1670558868588617975)
XLA Ops:
  0.0 30.2 %shard_map.64 = f32[2,512,256]{2,1,0:T(8,128)} custom-call(bf16[256,1024]{1,0:T(8,128)(2,1)} %frag_hbm.1, s32[1,256]{1,0:T(1,128)} %order_hbm.1, s32[1,256]{1,0:T(1,128)} %bitcast.5, bf16[1024,1024]{1,0:T(8,128)(2,1)} %w1_hbm.1, bf16[1024,256]{1,0:T(8,128)(2,1)} %w2_hbm.1, f32[2,512,256]{2,1,0:T(8,128)} %bitcast.4), custom_call_target="tpu_custom_call" | custom-call | tf_op jit(solution)/shard_map/pallas_call | solution.py:366
  30.2 2.3 %copy.8 = f32[1024,256]{1,0:T(8,128)} copy(f32[1024,256]{1,0:T(8,128)} %bitcast.3) | data formatting | bytes 2097152

commit v4 on v3

--- a/solution.py
+++ b/solution.py
@@ -359,7 +359,7 @@
     blocks = min(n_cent, 8)
     half = centroids.shape[0] // CORES
     n_tiles = hid // TILE
-    n_stat = n_dp * n_cent if n_dp * n_cent <= 32 else n_dp
+    n_stat = n_dp
     f32, bf16 = jnp.float32, jnp.bfloat16
     dma = pltpu.SemaphoreType.DMA
     hbm = pl.BlockSpec(memory_space=pltpu.HBM)

time: 32.6 us -> 31.3 us (0.960)
  Pallas kernels: 30.2 us -> 28.9 us
    pallas_call x1, Pallas kernels: 30.2 us -> 28.9 us  [per_device(): pl.pallas_call(functools.partial(kernel, n_dp, n_cent, cap, blocks), out_...]
where the time goes in v4:
time: 31.3 us; the launch traced here: 31.2 us
  Pallas kernels  28.9 us (92%)
  local copies, waits for them, and re-layouts  2.26 us (7%)
    pallas_call x1, Pallas kernels, per_device(): pl.pallas_call(functools.partial(kernel, n_dp, n_cent, cap, blocks), out_...  28.9 us
    unnamed x1, local copies, waits for them, and re-layouts  2.26 us

profile of v4, /device:TPU:0, one launch (start us, length us, event | category | flops | bytes accessed | tf_op | source)
XLA Modules:
  0.0 31.2 jit_solution(16274786867421334925)
XLA Ops:
  0.0 28.9 %shard_map.64 = f32[2,512,256]{2,1,0:T(8,128)} custom-call(bf16[256,1024]{1,0:T(8,128)(2,1)} %frag_hbm.1, s32[1,256]{1,0:T(1,128)} %order_hbm.1, s32[1,256]{1,0:T(1,128)} %bitcast.5, bf16[1024,1024]{1,0:T(8,128)(2,1)} %w1_hbm.1, bf16[1024,256]{1,0:T(8,128)(2,1)} %w2_hbm.1, f32[2,512,256]{2,1,0:T(8,128)} %bitcast.4), custom_call_target="tpu_custom_call" | custom-call | tf_op jit(solution)/shard_map/pallas_call | solution.py:366
  28.9 2.3 %copy.8 = f32[1024,256]{1,0:T(8,128)} copy(f32[1024,256]{1,0:T(8,128)} %bitcast.3) | data formatting | bytes 2097152
